TPU v7x, 32 devices: a whole 2x2x4 slice. The times are simulated.
32 devices in a mesh: groups: 2 (over y), tensor: 4 (over z), batch: 2 (over x), pool: 2 (over core).
Axes of the slice: x: 2, y: 2, z: 4, core: 2. Of those that a mesh axis runs over, the one named last changes fastest.
Arguments:
- hidden_input: bfloat16 [32, 4, 8192], P(('groups', 'tensor', 'batch', 'pool')), parts along dimension 0, may hold values from -6 to 6
- query_matrix: bfloat16 [8192, 4096], P(None, 'tensor'), may hold values from -0.0625 to 0.0625
- adapter_down_weight: bfloat16 [32, 64, 8192], P(('tensor', 'pool')), may hold values from -0.0625 to 0.0625
- adapter_up_weight: bfloat16 [32, 64, 4096], P(('tensor', 'pool')), may hold values from -0.75 to 0.75
- request_adapter: int32 [32], P(('groups', 'tensor', 'batch', 'pool')), parts along dimension 0, may hold values from 0 to 31
- adapter_slot: int32 [32], replicated, may hold values from 0 to 31, each once
- cached_key_value: bfloat16 [32, 2, 512, 512], P(('groups', 'tensor', 'batch', 'pool')), parts along dimension 0, may hold values from -610 to 610
- fresh_key_value: bfloat16 [32, 2, 4, 512], P(('groups', 'tensor', 'batch', 'pool')), parts along dimension 0, may hold values from -6 to 6
- cached_length: int32 [32], P(('groups', 'tensor', 'batch', 'pool')), parts along dimension 0, may hold values from 2 to 512, as said below
Outputs:
- attention_out: bfloat16 [32, 4, 4096], P(('groups', 'tensor', 'batch', 'pool')), parts along dimension 0
There are 2 independent parts, one for each index of `groups`. A program takes and returns all parts, laid end to end along the dimension named above; an argument that names none is the same for every part. Nothing has to cross between parts.
Inputs may be any that keep to these rules, and one draw needn't show every extreme that they name: Request r attends cached positions 0 to cached_length[r] - 1; some request has exactly 512.
All inputs are finite; a program needn't handle non-finite values.
Results may differ from a plain program's by a relative error of at most 0.012.
The roundings to bfloat16 on the way count: a program that leaves them out, or rounds other values in their place, can miss the bound.
Values may be sent and summed in bfloat16 or wider, within the bound.
A program may use at most 128 MiB of HBM per device.

v0:
```python
import math

import jax
import jax.numpy as jnp
from jax import lax
from jax.sharding import PartitionSpec as P

QUERY_HEADS = 32
KVH = 4
HEAD_WIDTH = 128


def attend(queries, cached_key_value, fresh_key_value, cached_length):
    req_count = queries.shape[0]
    step_count = queries.shape[1]
    cache_size = cached_key_value.shape[2]
    group_size = QUERY_HEADS // KVH
    head_rows = queries.reshape(req_count, step_count, KVH, group_size, HEAD_WIDTH)
    cache_keys = cached_key_value[:, 0].reshape(req_count, cache_size, KVH, HEAD_WIDTH)
    cache_values = cached_key_value[:, 1].reshape(req_count, cache_size, KVH, HEAD_WIDTH)
    new_keys = fresh_key_value[:, 0].reshape(req_count, step_count, KVH, HEAD_WIDTH)
    new_values = fresh_key_value[:, 1].reshape(req_count, step_count, KVH, HEAD_WIDTH)
    score_scale = 1.0 / math.sqrt(HEAD_WIDTH)
    cached_scores = (
        jnp.einsum("rskgd,rlkd->rkgsl", head_rows, cache_keys, preferred_element_type=jnp.float32)
        * score_scale
    )
    fresh_scores = (
        jnp.einsum("rskgd,rtkd->rkgst", head_rows, new_keys, preferred_element_type=jnp.float32)
        * score_scale
    )
    valid_old = (jnp.arange(cache_size, dtype=jnp.int32)[None, :] < cached_length[:, None])[
        :, None, None, None, :
    ]
    valid_new = (
        jnp.arange(step_count, dtype=jnp.int32)[None, :]
        <= jnp.arange(step_count, dtype=jnp.int32)[:, None]
    )[None, None, None]
    cached_scores = jnp.where(valid_old, cached_scores, -1e30)
    fresh_scores = jnp.where(valid_new, fresh_scores, -1e30)
    row_max = jnp.maximum(jnp.max(cached_scores, axis=-1), jnp.max(fresh_scores, axis=-1))[
        ..., None
    ]
    exp_cached = jnp.exp(cached_scores - row_max)
    exp_fresh = jnp.exp(fresh_scores - row_max)
    denominator = jnp.sum(exp_cached, axis=-1, keepdims=True) + jnp.sum(
        exp_fresh, axis=-1, keepdims=True
    )
    weight_cached = (exp_cached / denominator).astype(jnp.bfloat16)
    weight_fresh = (exp_fresh / denominator).astype(jnp.bfloat16)
    combined = jnp.einsum(
        "rkgsl,rlkd->rskgd", weight_cached, cache_values, preferred_element_type=jnp.float32
    )
    combined = combined + jnp.einsum(
        "rkgst,rtkd->rskgd", weight_fresh, new_values, preferred_element_type=jnp.float32
    )
    return combined.reshape(req_count, step_count, QUERY_HEADS * HEAD_WIDTH).astype(jnp.bfloat16)


def per_device(
    hidden_input,
    query_matrix,
    adapter_down_weight,
    adapter_up_weight,
    request_adapter,
    adapter_slot,
    cached_key_value,
    fresh_key_value,
    cached_length,
):
    req_dev = hidden_input.shape[0]
    step_count = hidden_input.shape[1]
    width_of_model = hidden_input.shape[2]
    tensor_count = lax.axis_size("tensor")
    n_pool = lax.axis_size("pool")
    tensor_idx = lax.axis_index("tensor")
    pool_idx = lax.axis_index("pool")
    slots_per_device = adapter_up_weight.shape[0]
    adapter_rank_size = adapter_up_weight.shape[1]
    head_column_block = query_matrix.shape[1]
    group_rows = tensor_count * req_dev * step_count
    gathered, group_ids = (
        lax.all_gather(hidden_input, ("tensor", "pool"), axis=0, tiled=True),
        lax.all_gather(request_adapter, ("tensor", "pool"), axis=0, tiled=True),
    )
    adapters = adapter_slot.shape[0]
    id_match = group_ids[:, None] == jnp.arange(adapters, dtype=jnp.int32)[None, :]
    row_slot = jnp.sum(jnp.where(id_match, adapter_slot[None, :], 0), axis=1)
    owner_index = tensor_idx * n_pool + pool_idx
    own_slots = owner_index * slots_per_device + jnp.arange(slots_per_device, dtype=jnp.int32)
    own_mask = (row_slot[:, None] == own_slots[None, :]).astype(jnp.float32)
    flat_rows = gathered.reshape(-1, width_of_model)
    down_flattened = adapter_down_weight.reshape(
        slots_per_device * adapter_rank_size, width_of_model
    )
    projected = lax.dot_general(
        flat_rows, down_flattened, (((1,), (1,)), ((), ())), preferred_element_type=jnp.float32
    )
    masked = (
        projected.reshape(-1, step_count, slots_per_device, adapter_rank_size)
        * own_mask[:, None, :, None]
    )
    base_rows = gathered.reshape(tensor_count, n_pool, req_dev * step_count, width_of_model)
    own_group = lax.dynamic_index_in_dim(base_rows, pool_idx, 1, keepdims=False).reshape(
        group_rows, width_of_model
    )
    base_query = jnp.dot(own_group, query_matrix, preferred_element_type=jnp.float32)
    low_rows = masked.astype(jnp.bfloat16).reshape(
        tensor_count, n_pool, req_dev * step_count, slots_per_device * adapter_rank_size
    )
    by_group = jnp.transpose(low_rows, (1, 0, 2, 3)).reshape(
        n_pool, group_rows, slots_per_device * adapter_rank_size
    )
    up_weight_blocks = adapter_up_weight.reshape(
        slots_per_device * adapter_rank_size, tensor_count, head_column_block
    )
    block_count = group_rows * lax.axis_size(("tensor", "pool")) // group_rows
    block_index = jnp.arange(block_count, dtype=jnp.int32)
    head_block = block_index // n_pool
    group_index = block_index % n_pool
    picked_rows = jnp.take(by_group, group_index, axis=0)
    picked_cols = jnp.take(up_weight_blocks, head_block, axis=1)
    partial_sum = jnp.einsum(
        "brk,kbc->brc", picked_rows, picked_cols, preferred_element_type=jnp.float32
    )
    low_delta = lax.psum_scatter(
        partial_sum.reshape(block_count * group_rows, head_column_block),
        ("tensor", "pool"),
        scatter_dimension=0,
        tiled=True,
    )
    queries = (base_query + low_delta).astype(jnp.bfloat16)
    regrouped = lax.all_to_all(
        queries.reshape(tensor_count, req_dev * step_count, head_column_block),
        "tensor",
        split_axis=0,
        concat_axis=2,
        tiled=True,
    )
    return attend(regrouped, cached_key_value, fresh_key_value, cached_length)


def solution(mesh):
    placed = (
        P(("groups", "tensor", "batch", "pool"), None, None),
        P(None, "tensor"),
        P(("tensor", "pool"), None, None),
        P(("tensor", "pool"), None, None),
        P(("groups", "tensor", "batch", "pool")),
        P(),
        P(("groups", "tensor", "batch", "pool"), None, None, None),
        P(("groups", "tensor", "batch", "pool"), None, None, None),
        P(("groups", "tensor", "batch", "pool")),
    )
    return jax.shard_map(
        per_device,
        mesh=mesh,
        in_specs=placed,
        out_specs=P(("groups", "tensor", "batch", "pool"), None, None),
        check_vma=False,
    )
```

profile of v0, /device:TPU:0, one launch (start us, length us, event | category | flops | bytes accessed | tf_op | source)
XLA Modules:
  0.0 108.7 jit_solution(7161985664319013350)
XLA Ops:
  6.6 16.8 %all_gather.6 = bf16[8,4,8192]{2,1,0:T(4,128)(2,1)S(1)} all-gather(bf16[1,4,8192]{2,1,0:T(4,128)(2,1)} %param.9), channel_id=1, replica_groups=mesh['groups'=2,'tensor'=4,'batch'=2,'pool'=2] {'tensor','pool'}, dimensions={0}, use_global_device_ids=true | all-gather | bytes 589824 | tf_op jit(solution)/shard_map/all_gather | solution.py:83
  24.0 1.2 %dynamic-slice = u32[1]{0:T(128)} dynamic-slice(u32[32]{0:T(128)} %constant.94, u32[]{:T(128)S(6)} %add.106), dynamic_slice_sizes={1} | dynamic-slice | bytes 12
  25.3 0.8 dynamic-update-slice
  26.0 8.9 %all-reduce = s32[8]{0:T(128)S(1)} all-reduce(s32[8]{0:T(128)S(1)} %dynamic-update-slice), channel_id=1, replica_groups=mesh['groups'=2,'tensor'=4,'batch'=2,'pool'=2] {'tensor','pool'}, use_global_device_ids=true, to_apply=%add | all-reduce | flops 8 | bytes 64
  34.9 0.8 select_reduce_fusion
  35.9 4.4 %fusion.14 = bf16[8,4,4,64]{3,1,2,0:T(4,128)(2,1)S(1)} fusion(bf16[4,64,8192]{2,1,0:T(8,128)(2,1)} %param.11, bf16[8,4,8192]{2,1,0:T(4,128)(2,1)S(1)} %all_gather.6, f32[8,4]{1,0:T(8,128)S(1)} %compare_convert_fusion), kind=kOutput, calls=%fused_computation.17 | convolution fusion | flops 134234112 | bytes 4735104 | tf_op jit(solution)/shard_map/dot_general | solution.py:96
  40.5 2.8 %reshape.255 = bf16[256,4,1024]{2,1,0:T(4,128)(2,1)} reshape(bf16[4,64,4096]{2,1,0:T(8,128)(2,1)S(1)} %copy-done) | data formatting | bytes 4194304 | tf_op jit(solution)/shard_map/reshape | solution.py:114
  43.3 2.2 %copy.47 = bf16[256,4,1024]{2,0,1:T(8,128)(2,1)S(1)} copy(bf16[256,4,1024]{2,1,0:T(4,128)(2,1)} %reshape.255) | data formatting | bytes 4194304 | tf_op jit(solution)/shard_map/reshape | solution.py:114
  45.5 0.6 gather_fusion
  46.1 2.7 %gather_fusion.1 = bf16[8,256,1024]{2,1,0:T(8,128)(2,1)} fusion(bf16[256,4,1024]{2,0,1:T(8,128)(2,1)S(1)} %copy.47, s32[1024]{0:T(1024)S(1)} %pad_clamp_fusion), kind=kCustom, calls=%fused_computation.1 | custom fusion | bytes 8388640 | tf_op jit(solution)/shard_map/jit(_take)/gather | solution.py:122
  48.8 3.9 %fusion = f32[8,16,1024]{2,1,0:T(8,128)} fusion(bf16[8,256,1024]{2,1,0:T(8,128)(2,1)} %gather_fusion.1, pred[8]{0:T(512)(128)(4,1)S(1)} %get-tuple-element.11, bf16[8,16,256]{2,1,0:T(8,128)(2,1)S(1)} %gather_fusion, pred[8]{0:T(512)(128)(4,1)S(1)} %get-tuple-element.12), kind=kOutput, calls=%fused_computation.2 | convolution fusion | flops 69238784 | bytes 4784144 | tf_op jit(solution)/shard_map/brk,kbc->brc/dot_general | solution.py:123
  53.6 28.6 %reduce-scatter.2.cloned.1.call-done = f32[16,1024]{1,0:T(8,128)} async-done(((f32[128,1024]{1,0:T(8,128)}), f32[16,1024]{1,0:T(8,128)}) %reduce-scatter.2.cloned.1.call-update) | async-done | bytes 65552 | tf_op jit(solution)/shard_map/reduce_scatter | solution.py:126
  82.2 8.0 %fusion.17 = bf16[16,1024]{1,0:T(8,128)(2,1)S(1)} fusion(f32[16,1024]{1,0:T(8,128)} %reduce-scatter.2.cloned.1.call-done, bf16[16,8192]{1,0:T(8,128)(2,1)S(1)} %reshape.252, bf16[8192,1024]{1,0:T(8,128)(2,1)} %param.10), kind=kOutput, calls=%fused_computation.18 | convolution fusion | flops 268468224 | bytes 17137664 | tf_op jit(solution)/shard_map/dot_general | solution.py:107
  90.3 0.6 reshape.257
  90.9 3.3 %all-to-all-start = ((bf16[4,4,1024]{2,1,0:T(4,128)(2,1)}), bf16[4,4,1024]{2,1,0:T(4,128)(2,1)S(1)}, u32[]{:S(2)}, u32[]{:S(2)}) async-start(bf16[4,4,1024]{2,1,0:T(4,128)(2,1)} %reshape.257), calls=%async_computation.1 | async-start | bytes 65536 | tf_op jit(solution)/shard_map/all_to_all | solution.py:133
  94.2 0.2 copy.63
  94.4 0.2 copy.64
  94.7 5.2 %all-to-all-done = bf16[4,4,1024]{2,1,0:T(4,128)(2,1)S(1)} async-done(((bf16[4,4,1024]{2,1,0:T(4,128)(2,1)}), bf16[4,4,1024]{2,1,0:T(4,128)(2,1)S(1)}, u32[]{:S(2)}, u32[]{:S(2)}) %all-to-all-start) | async-done | bytes 32800 | tf_op jit(solution)/shard_map/all_to_all | solution.py:133
  99.8 0.3 fusion.40
  100.1 0.3 fusion.41
  100.4 0.2 fusion.22
  100.7 0.3 fusion.23
  101.0 0.2 fusion.18
  101.2 0.6 convert_element_type.51
  (30 shorter events, 0.6 us)
Async XLA Ops:
  6.5 75.7 %reduce-scatter.2.cloned.1.call-start = ((), (), s32[]{:S(2)}) async-start(), calls=%async_computation.2 | async-start | bytes 589824 | tf_op jit(solution)/shard_map/reduce_scatter | solution.py:126
  35.9 4.6 %copy-start = (bf16[4,64,4096]{2,1,0:T(8,128)(2,1)S(1)}, bf16[4,64,4096]{2,1,0:T(8,128)(2,1)}, u32[]{:S(2)}) copy-start(bf16[4,64,4096]{2,1,0:T(8,128)(2,1)} %param.12) | copy-start | bytes 6291460
  48.8 4.7 %copy-start.1 = (bf16[1,2,512,512]{3,2,1,0:T(8,128)(2,1)S(1)}, bf16[1,2,512,512]{3,2,1,0:T(8,128)(2,1)}, u32[]{:S(2)}) copy-start(bf16[1,2,512,512]{3,2,1,0:T(8,128)(2,1)} %param.15) | copy-start | bytes 3145732
  53.6 46.5 %copy-start.2 = (bf16[1,2,4,512]{3,2,1,0:T(4,128)(2,1)S(1)}, bf16[1,2,4,512]{3,2,1,0:T(4,128)(2,1)}, u32[]{:S(2)}) copy-start(bf16[1,2,4,512]{3,2,1,0:T(4,128)(2,1)} %param.16) | copy-start | bytes 24580
  90.9 8.9 %all-to-all-start = ((bf16[4,4,1024]{2,1,0:T(4,128)(2,1)}), bf16[4,4,1024]{2,1,0:T(4,128)(2,1)S(1)}, u32[]{:S(2)}, u32[]{:S(2)}) async-start(bf16[4,4,1024]{2,1,0:T(4,128)(2,1)} %reshape.257), calls=%async_computation.1 | async-start | bytes 65536 | tf_op jit(solution)/shard_map/all_to_all | solution.py:133
Sparse Core Ops, SparseCore 0:
  52.8 29.4 reduce-scatter.1
where the time goes:
time: 109 us
  waiting for transfers between devices  33.8 us (31%)
  blocking collectives  25.7 us (24%)
  matrix products  17.4 us (16%)
  between operations  14.9 us (14%)
  local copies, waits for them, and re-layouts  12.4 us (11%)
  starting transfers between devices  3.27 us (3%)
  other arithmetic  1.22 us (1%)
    reduce_scatter x1, waiting for transfers between devices, per_device(): lax.psum_scatter(partial_sum.reshape(block_count * group_rows, head_colum...  28.6 us
    all_gather x1, blocking collectives, per_device(): lax.all_gather(hidden_input, ('tensor', 'pool'), axis=0, tiled=True)  16.8 us
    unnamed x1, blocking collectives  8.93 us
    dot_general x1, matrix products, per_device(): jnp.dot(own_group, query_matrix, preferred_element_type=jnp.float32)  8.04 us
    all_to_all x1, waiting for transfers between devices, per_device(): lax.all_to_all(queries.reshape(tensor_count, req_dev * step_count, head_c...  5.18 us
    reshape x2, local copies, waits for them, and re-layouts, per_device(): adapter_up_weight.reshape(slots_per_device * adapter_rank_size, tensor_co...  5.01 us
    dot_general x1, matrix products, per_device(): lax.dot_general(flat_rows, down_flattened, (((1,), (1,)), ((), ())), pref...  4.41 us
    dot_general x1, matrix products, per_device(): jnp.einsum('brk,kbc->brc', picked_rows, picked_cols, preferred_element_ty...  3.85 us
  transfers between devices with their start and end apart: 2, of which 2 were waited for; matrix products, arithmetic and copies ran while one was open for 1% of the time, Pallas kernels for 0%

commit v1 on v0

--- a/solution.py
+++ b/solution.py
@@ -1,13 +1,21 @@
+import functools
 import math
+from typing import NamedTuple
 
 import jax
 import jax.numpy as jnp
 from jax import lax
+from jax.experimental import pallas as pl
+from jax.experimental.pallas import tpu as pltpu
 from jax.sharding import PartitionSpec as P
 
 QUERY_HEADS = 32
 KVH = 4
 HEAD_WIDTH = 128
+CHUNKS = 2
+LINK = jnp.float32
+LINK_SCALE = 1.0
+MESH = pl.DeviceIdType.MESH
 
 
 def attend(queries, cached_key_value, fresh_key_value, cached_length):
@@ -139,6 +147,322 @@
     )
     return attend(regrouped, cached_key_value, fresh_key_value, cached_length)
 
+def fused(
+    dims,
+    hidden_ref, matrix_ref, down_ref, up_ref, adapter_ref, table_ref, cache_ref, fresh_ref, length_ref,
+    out_ref,
+    gath, matrix_v, down_v, up_v, cache_v, hidden_v, fresh_v, adapter_s, table_s, length_s, slots,
+    exch_out, exch_in, delta_out, delta_in, base_out, base_in,
+    load_sem, small_sem, z_send, z_recv, f_send, f_recv, s_send, s_recv,
+    x_send, x_recv, d_send, d_recv, b_send, b_recv,
+):
+    T, NC = dims.tensor, dims.chunks
+    R = 2 * T
+    steps, width = hidden_ref.shape[1], hidden_ref.shape[2]
+    rows = R * steps
+    part = width // NC
+    lanes = part // 4
+    half = matrix_v.shape[1]
+    span = half * 2
+    slot_count, rank = down_ref.shape[0], down_ref.shape[1]
+    kvw = cache_ref.shape[3]
+    cache_size = cache_ref.shape[2]
+    t = lax.axis_index("tensor")
+    p = lax.axis_index("pool")
+    other = 1 - p
+    me = t * 2 + p
+
+    def up_t(j):
+        return lax.rem(t + j, T)
+
+    def down_t(j):
+        return lax.rem(t + T - j, T)
+
+    def remote(src, dst, ssem, rsem, tt, pp):
+        return pltpu.make_async_remote_copy(
+            src_ref=src, dst_ref=dst, send_sem=ssem, recv_sem=rsem,
+            device_id={"tensor": tt, "pool": pp}, device_id_type=MESH,
+        )
+
+    smalls = [
+        pltpu.make_async_copy(src, dst, small_sem.at[n])
+        for n, (src, dst) in enumerate(
+            (
+                (hidden_ref.at[0], hidden_v),
+                (adapter_ref, adapter_s),
+                (table_ref, table_s),
+                (fresh_ref.at[0], fresh_v),
+                (length_ref, length_s),
+            )
+        )
+    ]
+    for load in smalls:
+        load.start()
+    mat_cols = pl.ds(pl.multiple_of(p * half, half), half)
+    mat_loads, down_loads = [], []
+    for c in range(NC):
+        ks = pl.ds(c * part, part)
+        mat_loads.append(pltpu.make_async_copy(matrix_ref.at[ks, mat_cols], matrix_v.at[ks], load_sem.at[2 * c]))
+        down_loads.append(pltpu.make_async_copy(down_ref.at[:, :, ks], down_v.at[:, :, ks], load_sem.at[2 * c + 1]))
+        mat_loads[c].start()
+        down_loads[c].start()
+    up_load = pltpu.make_async_copy(up_ref, up_v, load_sem.at[2 * NC])
+    cache_load = pltpu.make_async_copy(cache_ref.at[0], cache_v, load_sem.at[2 * NC + 1])
+    up_load.start()
+    cache_load.start()
+
+    barrier = pltpu.get_barrier_semaphore()
+    for j in range(T):
+        for q in range(2):
+            if j or q:
+                pl.semaphore_signal(
+                    barrier, inc=1, device_id={"tensor": up_t(j), "pool": other if q else p}, device_id_type=MESH
+                )
+
+    smalls[0].wait()
+    own = hidden_v[...].astype(jnp.float32)
+    for c in range(NC):
+        pieces = [own[:, c * part + q * lanes : c * part + (q + 1) * lanes] for q in range(4)]
+        gath[c, 0] = jnp.concatenate(pieces, axis=0).astype(jnp.bfloat16)
+    smalls[1].wait()
+    smalls[2].wait()
+    slots[0] = jnp.full((8, 128), table_s[adapter_s[0]], jnp.int32)
+
+    pl.semaphore_wait(barrier, R - 1)
+
+    pending = []
+    zc, fc = {}, {}
+    for c in range(NC):
+        for j in range(1, T):
+            zc[c, j] = remote(gath.at[c, 0], gath.at[c, 2 * j], z_send.at[c, j], z_recv.at[c, j], up_t(j), p)
+            zc[c, j].start()
+            pending.append(zc[c, j])
+        for j in range(T):
+            fc[c, j] = remote(gath.at[c, 2 * j], gath.at[c, 2 * j + 1], f_send.at[c, j], f_recv.at[c, j], t, other)
+            pending.append(fc[c, j])
+        fc[c, 0].start()
+    sc = []
+    for r in range(1, R):
+        s = remote(slots.at[0], slots.at[r], s_send.at[r], s_recv.at[r], up_t(r // 2), other if r % 2 else p)
+        s.start()
+        sc.append(s)
+        pending.append(s)
+
+    i0 = lax.broadcasted_iota(jnp.int32, (4 * rows, 4 * rows), 0)
+    i1 = lax.broadcasted_iota(jnp.int32, (4 * rows, 4 * rows), 1)
+    q0 = lax.div(i0, rows)
+    r0 = lax.div(lax.rem(i0, rows), steps)
+    s0 = lax.rem(i0, steps)
+    order = jnp.where(i1 == r0 * (4 * steps) + q0 * steps + s0, 1.0, 0.0).astype(jnp.bfloat16)
+
+    smalls[3].wait()
+    smalls[4].wait()
+    fresh = fresh_v[...].astype(jnp.float32)
+    pad = jnp.zeros((128 - steps, kvw), jnp.float32)
+    fresh_keys = jnp.concatenate([fresh[0], pad], axis=0).astype(jnp.bfloat16)
+    fresh_vals = jnp.concatenate([fresh[1], pad], axis=0).astype(jnp.bfloat16)
+
+    base = jnp.zeros((rows, half), jnp.float32)
+    low_t = jnp.zeros((slot_count * rank, rows), jnp.float32)
+    for c in range(NC):
+        for j in range(1, T):
+            zc[c, j].wait_recv()
+            fc[c, j].start()
+        for j in range(T):
+            fc[c, j].wait_recv()
+        mat_loads[c].wait()
+        down_loads[c].wait()
+        arrived = gath[c].reshape(R * 4 * steps, lanes)
+        ordered = jnp.dot(order, arrived, preferred_element_type=jnp.float32).astype(jnp.bfloat16)
+        for q in range(4):
+            lhs = ordered[q * rows : (q + 1) * rows]
+            k0 = c * part + q * lanes
+            dn = down_v[:, :, k0 : k0 + lanes].reshape(slot_count * rank, lanes)
+            low_t += lax.dot_general(dn, lhs, (((1,), (1,)), ((), ())), preferred_element_type=jnp.float32)
+            base += jnp.dot(lhs, matrix_v[k0 : k0 + lanes, :], preferred_element_type=jnp.float32)
+
+    h2 = half // 2
+    bc = []
+    for r in range(R):
+        rb = base[r * steps : (r + 1) * steps]
+        block = jnp.concatenate([rb[:, :h2], rb[:, h2:]], axis=0)
+        if r == 0:
+            base_in[me] = block
+        else:
+            base_out[r] = block
+            tt, pp = down_t(r // 2), (other if r % 2 else p)
+            b = remote(base_out.at[r], base_in.at[me], b_send.at[r], b_recv.at[r], tt, pp)
+            b.start()
+            bc.append(b)
+
+    for s in sc:
+        s.wait_recv()
+    ri = lax.broadcasted_iota(jnp.int32, (rows, 128), 0)
+    row_slot = jnp.zeros((rows, 128), jnp.int32)
+    for r in range(R):
+        here = (ri >= r * steps) & (ri < (r + 1) * steps)
+        row_slot = jnp.where(here, jnp.broadcast_to(slots[r, 0:1, :], (rows, 128)), row_slot)
+    low = low_t.T
+    bits = []
+    for n in range(slot_count * rank // 128):
+        col_slot = me * slot_count + lax.div(lax.broadcasted_iota(jnp.int32, (rows, 128), 1) + n * 128, rank)
+        bits.append(jnp.where(row_slot == col_slot, low[:, n * 128 : (n + 1) * 128], 0.0))
+    low = jnp.concatenate(bits, axis=1).astype(jnp.bfloat16)
+
+    up_load.wait()
+    deltas = []
+    for k in range(T):
+        upk = up_v[:, :, k * span : (k + 1) * span].reshape(slot_count * rank, span)
+        deltas.append(jnp.dot(low, upk, preferred_element_type=jnp.float32))
+
+    def block_of(r):
+        return jnp.concatenate([d[r * steps : (r + 1) * steps] for d in deltas], axis=0)
+
+    order_j = list(range(1, T)) + [0]
+    xc, dc = {}, {}
+    for j in order_j:
+        exch_out[j] = (block_of(2 * j + 1) * LINK_SCALE).astype(LINK)
+        xc[j] = remote(exch_out.at[j], exch_in.at[j], x_send.at[j], x_recv.at[j], t, other)
+        xc[j].start()
+        pending.append(xc[j])
+    mine = {j: block_of(2 * j) for j in order_j}
+    for j in order_j:
+        xc[j].wait_recv()
+        both = mine[j] * LINK_SCALE + exch_in[j].astype(jnp.float32)
+        if j:
+            delta_out[j] = both.astype(LINK)
+            dc[j] = remote(delta_out.at[j], delta_in.at[j], d_send.at[j], d_recv.at[j], down_t(j), p)
+            dc[j].start()
+            pending.append(dc[j])
+        else:
+            total = both
+
+    cache_load.wait()
+    for b in bc:
+        b.wait_recv()
+    parts = []
+    for tt in range(T):
+        pieces = []
+        for pp in range(2):
+            got = base_in[tt * 2 + pp]
+            pieces += [got[:steps], got[steps:]]
+        parts.append(jnp.concatenate(pieces, axis=1))
+    base_rows = jnp.concatenate(parts, axis=0)
+    for j in range(1, T):
+        dc[j].wait_recv()
+        total = total + delta_in[j].astype(jnp.float32)
+    queries = (base_rows + total * (1.0 / LINK_SCALE)).astype(jnp.bfloat16).astype(jnp.float32)
+
+    groups = span // HEAD_WIDTH
+    heads = groups * steps
+    scale = 1.0 / math.sqrt(HEAD_WIDTH)
+    length = length_s[0]
+    old_ok = lax.broadcasted_iota(jnp.int32, (heads, cache_size), 1) < length
+    step_of = lax.rem(lax.broadcasted_iota(jnp.int32, (heads, 128), 0), steps)
+    new_ok = lax.broadcasted_iota(jnp.int32, (heads, 128), 1) <= step_of
+    nt = (((1,), (1,)), ((), ()))
+    for k in range(T):
+        rows_k = queries[k * steps : (k + 1) * steps]
+        qk = jnp.concatenate(
+            [rows_k[:, g * HEAD_WIDTH : (g + 1) * HEAD_WIDTH] for g in range(groups)], axis=0
+        ).astype(jnp.bfloat16)
+        cols = slice(k * HEAD_WIDTH, (k + 1) * HEAD_WIDTH)
+        old = lax.dot_general(qk, cache_v[0, :, cols], nt, preferred_element_type=jnp.float32) * scale
+        new = lax.dot_general(qk, fresh_keys[:, cols], nt, preferred_element_type=jnp.float32) * scale
+        old = jnp.where(old_ok, old, -1e30)
+        new = jnp.where(new_ok, new, -1e30)
+        top = jnp.maximum(jnp.max(old, axis=1, keepdims=True), jnp.max(new, axis=1, keepdims=True))
+        old = jnp.exp(old - top)
+        new = jnp.exp(new - top)
+        den = jnp.sum(old, axis=1, keepdims=True) + jnp.sum(new, axis=1, keepdims=True)
+        inv = 1.0 / den
+        res = jnp.dot((old * inv).astype(jnp.bfloat16), cache_v[1, :, cols], preferred_element_type=jnp.float32)
+        res += jnp.dot((new * inv).astype(jnp.bfloat16), fresh_vals[:, cols], preferred_element_type=jnp.float32)
+        flat = jnp.concatenate([res[g * steps : (g + 1) * steps] for g in range(groups)], axis=1)
+        out_ref[0, :, k * span : (k + 1) * span] = flat.astype(jnp.bfloat16)
+
+    for x in pending + bc:
+        x.wait_send()
+
+
+class Dims(NamedTuple):
+    tensor: int
+    chunks: int
+
+
+def fused_call(
+    hidden_input, query_matrix, adapter_down_weight, adapter_up_weight,
+    request_adapter, adapter_slot, cached_key_value, fresh_key_value, cached_length,
+):
+    T = lax.axis_size("tensor")
+    NC = CHUNKS
+    R = 2 * T
+    steps, width = hidden_input.shape[1], hidden_input.shape[2]
+    lanes = width // NC // 4
+    half = query_matrix.shape[1] // 2
+    span = half * 2
+    bf, f32 = jnp.bfloat16, jnp.float32
+    V, S = pltpu.VMEM, pltpu.SemaphoreType.DMA
+    vm, hb = (pl.BlockSpec(memory_space=m) for m in (pltpu.VMEM, pl.ANY))
+    M = pltpu.SMEM
+    return pl.pallas_call(
+        functools.partial(fused, Dims(T, NC)),
+        out_shape=jax.ShapeDtypeStruct((1, steps, span * T), bf),
+        in_specs=[hb] * 9,
+        out_specs=vm,
+        scratch_shapes=[
+            V((NC, R, 4 * steps, lanes), bf),
+            V((width, half), bf),
+            V(adapter_down_weight.shape, bf),
+            V(adapter_up_weight.shape, bf),
+            V(cached_key_value.shape[1:], bf),
+            V(hidden_input.shape[1:], bf),
+            V(fresh_key_value.shape[1:], bf),
+            M((1,), jnp.int32),
+            M(adapter_slot.shape, jnp.int32),
+            M((1,), jnp.int32),
+            V((R, 8, 128), jnp.int32),
+            V((T, T * steps, span), LINK),
+            V((T, T * steps, span), LINK),
+            V((T, T * steps, span), LINK),
+            V((T, T * steps, span), LINK),
+            V((R, 2 * steps, half // 2), f32),
+            V((R, 2 * steps, half // 2), f32),
+            S((2 * NC + 2,)),
+            S((5,)),
+            S((NC, T)), S((NC, T)), S((NC, T)), S((NC, T)),
+            S((R,)), S((R,)),
+            S((T,)), S((T,)), S((T,)), S((T,)),
+            S((R,)), S((R,)),
+        ],
+        compiler_params=pltpu.CompilerParams(
+            collective_id=0, has_side_effects=True, vmem_limit_bytes=62 * 1024 * 1024
+        ),
+        cost_estimate=pl.CostEstimate(flops=10**9, bytes_accessed=16 * 10**6, transcendentals=10**5),
+    )(
+        hidden_input, query_matrix, adapter_down_weight, adapter_up_weight,
+        request_adapter, adapter_slot, cached_key_value, fresh_key_value, cached_length,
+    )
+
+
+def fits_fused(hidden, matrix, down, cache):
+    return (
+        lax.axis_size("tensor") == KVH
+        and lax.axis_size("pool") == 2
+        and hidden.shape[0] == 1
+        and hidden.shape[1] == 4
+        and matrix.shape[1] == QUERY_HEADS // KVH * HEAD_WIDTH
+        and (down.shape[0] * down.shape[1]) % 128 == 0
+        and hidden.shape[2] % (CHUNKS * 4 * 128) == 0
+        and cache.shape[2] % 128 == 0
+    )
+
+def either(*arrays):
+    hidden, matrix, down, cache = arrays[0], arrays[1], arrays[2], arrays[6]
+    if fits_fused(hidden, matrix, down, cache):
+        return fused_call(*arrays)
+    return per_device(*arrays)
+
 
 def solution(mesh):
     placed = (
@@ -153,7 +477,7 @@
         P(("groups", "tensor", "batch", "pool")),
     )
     return jax.shard_map(
-        per_device,
+        either,
         mesh=mesh,
         in_specs=placed,
         out_specs=P(("groups", "tensor", "batch", "pool"), None, None),

time: 109 us -> 30.5 us (0.28)
  waiting for transfers between devices: 33.8 us -> 0 us
  Pallas kernels: 0 us -> 27.6 us
  blocking collectives: 25.7 us -> 0 us
  matrix products: 17.4 us -> 0 us
  between operations: 14.9 us -> 1.3 us
  local copies, waits for them, and re-layouts: 12.4 us -> 1.39 us
  starting transfers between devices: 3.27 us -> 0 us
  other arithmetic: 1.22 us -> 0 us
    reduce_scatter x1 -> x0, waiting for transfers between devices: 28.6 us -> none  [per_device(): lax.psum_scatter(partial_sum.reshape(block_count * group_rows, head_colum...]
    pallas_call x0 -> x1, Pallas kernels: none -> 27.6 us  [fused_call(): pl.pallas_call(functools.partial(fused, Dims(T, NC)), out_shape=jax.Shape...]
    dot_general x7 -> x0, matrix products: 17.4 us -> none  [the longest x1 8.04 us: per_device(): jnp.dot(own_group, query_matrix, preferred_element_type=jnp.float32)]
    all_gather x1 -> x0, blocking collectives: 16.8 us -> none  [per_device(): lax.all_gather(hidden_input, ('tensor', 'pool'), axis=0, tiled=True)]
    unnamed x1 -> x0, blocking collectives: 8.93 us -> none
    reshape x6 -> x0, local copies, waits for them, and re-layouts: 5.82 us -> none  [the longest x2 5.01 us: per_device(): adapter_up_weight.reshape(slots_per_device * adapter_rank_size, tensor_co...]
    all_to_all x1 -> x0, waiting for transfers between devices: 5.18 us -> none  [per_device(): lax.all_to_all(queries.reshape(tensor_count, req_dev * step_count, head_c...]
    gather x2 -> x0, local copies, waits for them, and re-layouts: 3.29 us -> none  [the longest x1 2.74 us: per_device(): picked_cols = jnp.take(up_weight_blocks, head_block, axis=1)]
  transfers between devices with their start and end apart: 2 -> 0, of which waited for: 2 -> 0; matrix products, arithmetic and copies ran while one was open for 1% -> 0% of each run, Pallas kernels for 0% -> 0%
where the time goes in v1:
time: 30.5 us; the launch traced here: 30.3 us
  Pallas kernels  27.6 us (90%)
  local copies, waits for them, and re-layouts  1.39 us (5%)
  between operations  1.3 us (4%)
    pallas_call x1, Pallas kernels, fused_call(): pl.pallas_call(functools.partial(fused, Dims(T, NC)), out_shape=jax.Shape...  27.6 us
    unnamed x1, local copies, waits for them, and re-layouts  1.39 us

profile of v1, /device:TPU:0, one launch (start us, length us, event | category | flops | bytes accessed | tf_op | source)
XLA Modules:
  0.0 30.3 jit_solution(7508308654886733049)
XLA Ops:
  1.3 27.6 %shard_map.91 = bf16[1,4,4096]{2,1,0:T(4,128)(2,1)} custom-call(bf16[1,4,8192]{2,1,0:T(4,128)(2,1)} %hidden_ref.1, bf16[8192,1024]{1,0:T(8,128)(2,1)} %matrix_ref.1, bf16[4,64,8192]{2,1,0:T(8,128)(2,1)} %down_ref.1, bf16[4,64,4096]{2,1,0:T(8,128)(2,1)} %up_ref.1, s32[1]{0:T(128)S(6)} %copy.11.adapter_ref, s32[32]{0:T(128)} %table_ref.1, ...), custom_call_target="tpu_custom_call" | custom-call | flops 1000000000 | bytes 16000000 | tf_op jit(solution)/shard_map/pallas_call | solution.py:408
  28.9 1.4 %copy.13 = bf16[1,4,4096]{2,1,0:T(4,128)(2,1)} copy(bf16[1,4,4096]{2,1,0:T(4,128)(2,1)} %shard_map.91) | data formatting | bytes 65536

commit v2 on v1

--- a/solution.py
+++ b/solution.py
@@ -14,7 +14,6 @@
 HEAD_WIDTH = 128
 CHUNKS = 2
 LINK = jnp.float32
-LINK_SCALE = 1.0
 MESH = pl.DeviceIdType.MESH
 
 
@@ -151,10 +150,10 @@
     dims,
     hidden_ref, matrix_ref, down_ref, up_ref, adapter_ref, table_ref, cache_ref, fresh_ref, length_ref,
     out_ref,
-    gath, matrix_v, down_v, up_v, cache_v, hidden_v, fresh_v, adapter_s, table_s, length_s, slots,
-    exch_out, exch_in, delta_out, delta_in, base_out, base_in,
-    load_sem, small_sem, z_send, z_recv, f_send, f_recv, s_send, s_recv,
-    x_send, x_recv, d_send, d_recv, b_send, b_recv,
+    gath, matrix_v, down_v, up_v, cache_v, hidden_v, fresh_v, adapter_s, table_s, length_s,
+    exch_out, exch_in, delta_out, delta_in,
+    load_sem, small_sem, z_send, z_recv, f_send, f_recv,
+    x_send, x_recv, d_send, d_recv,
 ):
     T, NC = dims.tensor, dims.chunks
     R = 2 * T
@@ -223,10 +222,12 @@
     own = hidden_v[...].astype(jnp.float32)
     for c in range(NC):
         pieces = [own[:, c * part + q * lanes : c * part + (q + 1) * lanes] for q in range(4)]
-        gath[c, 0] = jnp.concatenate(pieces, axis=0).astype(jnp.bfloat16)
+        gath[c, 0, :, :lanes] = jnp.concatenate(pieces, axis=0).astype(jnp.bfloat16)
     smalls[1].wait()
     smalls[2].wait()
-    slots[0] = jnp.full((8, 128), table_s[adapter_s[0]], jnp.int32)
+    slot_block = jnp.full((4 * steps, 128), table_s[adapter_s[0]], jnp.int32).astype(jnp.float32).astype(jnp.bfloat16)
+    for c in range(NC):
+        gath[c, 0, :, lanes:] = slot_block
 
     pl.semaphore_wait(barrier, R - 1)
 
@@ -241,13 +242,6 @@
             fc[c, j] = remote(gath.at[c, 2 * j], gath.at[c, 2 * j + 1], f_send.at[c, j], f_recv.at[c, j], t, other)
             pending.append(fc[c, j])
         fc[c, 0].start()
-    sc = []
-    for r in range(1, R):
-        s = remote(slots.at[0], slots.at[r], s_send.at[r], s_recv.at[r], up_t(r // 2), other if r % 2 else p)
-        s.start()
-        sc.append(s)
-        pending.append(s)
-
     i0 = lax.broadcasted_iota(jnp.int32, (4 * rows, 4 * rows), 0)
     i1 = lax.broadcasted_iota(jnp.int32, (4 * rows, 4 * rows), 1)
     q0 = lax.div(i0, rows)
@@ -272,7 +266,7 @@
             fc[c, j].wait_recv()
         mat_loads[c].wait()
         down_loads[c].wait()
-        arrived = gath[c].reshape(R * 4 * steps, lanes)
+        arrived = gath[c, :, :, :lanes].reshape(R * 4 * steps, lanes)
         ordered = jnp.dot(order, arrived, preferred_element_type=jnp.float32).astype(jnp.bfloat16)
         for q in range(4):
             lhs = ordered[q * rows : (q + 1) * rows]
@@ -281,39 +275,25 @@
             low_t += lax.dot_general(dn, lhs, (((1,), (1,)), ((), ())), preferred_element_type=jnp.float32)
             base += jnp.dot(lhs, matrix_v[k0 : k0 + lanes, :], preferred_element_type=jnp.float32)
 
-    h2 = half // 2
-    bc = []
-    for r in range(R):
-        rb = base[r * steps : (r + 1) * steps]
-        block = jnp.concatenate([rb[:, :h2], rb[:, h2:]], axis=0)
-        if r == 0:
-            base_in[me] = block
-        else:
-            base_out[r] = block
-            tt, pp = down_t(r // 2), (other if r % 2 else p)
-            b = remote(base_out.at[r], base_in.at[me], b_send.at[r], b_recv.at[r], tt, pp)
-            b.start()
-            bc.append(b)
-
-    for s in sc:
-        s.wait_recv()
     ri = lax.broadcasted_iota(jnp.int32, (rows, 128), 0)
-    row_slot = jnp.zeros((rows, 128), jnp.int32)
+    row_slot = jnp.zeros((rows, 128), jnp.float32)
     for r in range(R):
         here = (ri >= r * steps) & (ri < (r + 1) * steps)
-        row_slot = jnp.where(here, jnp.broadcast_to(slots[r, 0:1, :], (rows, 128)), row_slot)
+        row_slot = jnp.where(here, jnp.broadcast_to(gath[0, r, :, lanes:].astype(jnp.float32)[0:1], (rows, 128)), row_slot)
     low = low_t.T
     bits = []
     for n in range(slot_count * rank // 128):
         col_slot = me * slot_count + lax.div(lax.broadcasted_iota(jnp.int32, (rows, 128), 1) + n * 128, rank)
-        bits.append(jnp.where(row_slot == col_slot, low[:, n * 128 : (n + 1) * 128], 0.0))
+        bits.append(jnp.where(row_slot == col_slot.astype(jnp.float32), low[:, n * 128 : (n + 1) * 128], 0.0))
     low = jnp.concatenate(bits, axis=1).astype(jnp.bfloat16)
 
     up_load.wait()
+    base_wide = jnp.concatenate([jnp.where(p == 0, base, 0.0), jnp.where(p == 1, base, 0.0)], axis=1)
     deltas = []
     for k in range(T):
         upk = up_v[:, :, k * span : (k + 1) * span].reshape(slot_count * rank, span)
-        deltas.append(jnp.dot(low, upk, preferred_element_type=jnp.float32))
+        delta = jnp.dot(low, upk, preferred_element_type=jnp.float32)
+        deltas.append(delta + jnp.where(t == k, base_wide, 0.0))
 
     def block_of(r):
         return jnp.concatenate([d[r * steps : (r + 1) * steps] for d in deltas], axis=0)
@@ -321,14 +301,14 @@
     order_j = list(range(1, T)) + [0]
     xc, dc = {}, {}
     for j in order_j:
-        exch_out[j] = (block_of(2 * j + 1) * LINK_SCALE).astype(LINK)
+        exch_out[j] = (block_of(2 * j + 1)).astype(LINK)
         xc[j] = remote(exch_out.at[j], exch_in.at[j], x_send.at[j], x_recv.at[j], t, other)
         xc[j].start()
         pending.append(xc[j])
     mine = {j: block_of(2 * j) for j in order_j}
     for j in order_j:
         xc[j].wait_recv()
-        both = mine[j] * LINK_SCALE + exch_in[j].astype(jnp.float32)
+        both = mine[j] + exch_in[j].astype(jnp.float32)
         if j:
             delta_out[j] = both.astype(LINK)
             dc[j] = remote(delta_out.at[j], delta_in.at[j], d_send.at[j], d_recv.at[j], down_t(j), p)
@@ -338,20 +318,10 @@
             total = both
 
     cache_load.wait()
-    for b in bc:
-        b.wait_recv()
-    parts = []
-    for tt in range(T):
-        pieces = []
-        for pp in range(2):
-            got = base_in[tt * 2 + pp]
-            pieces += [got[:steps], got[steps:]]
-        parts.append(jnp.concatenate(pieces, axis=1))
-    base_rows = jnp.concatenate(parts, axis=0)
     for j in range(1, T):
         dc[j].wait_recv()
         total = total + delta_in[j].astype(jnp.float32)
-    queries = (base_rows + total * (1.0 / LINK_SCALE)).astype(jnp.bfloat16).astype(jnp.float32)
+    queries = total.astype(jnp.bfloat16).astype(jnp.float32)
 
     groups = span // HEAD_WIDTH
     heads = groups * steps
@@ -381,7 +351,7 @@
         flat = jnp.concatenate([res[g * steps : (g + 1) * steps] for g in range(groups)], axis=1)
         out_ref[0, :, k * span : (k + 1) * span] = flat.astype(jnp.bfloat16)
 
-    for x in pending + bc:
+    for x in pending:
         x.wait_send()
 
 
@@ -411,7 +381,7 @@
         in_specs=[hb] * 9,
         out_specs=vm,
         scratch_shapes=[
-            V((NC, R, 4 * steps, lanes), bf),
+            V((NC, R, 4 * steps, lanes + 128), bf),
             V((width, half), bf),
             V(adapter_down_weight.shape, bf),
             V(adapter_up_weight.shape, bf),
@@ -421,19 +391,14 @@
             M((1,), jnp.int32),
             M(adapter_slot.shape, jnp.int32),
             M((1,), jnp.int32),
-            V((R, 8, 128), jnp.int32),
             V((T, T * steps, span), LINK),
             V((T, T * steps, span), LINK),
             V((T, T * steps, span), LINK),
             V((T, T * steps, span), LINK),
-            V((R, 2 * steps, half // 2), f32),
-            V((R, 2 * steps, half // 2), f32),
             S((2 * NC + 2,)),
             S((5,)),
             S((NC, T)), S((NC, T)), S((NC, T)), S((NC, T)),
-            S((R,)), S((R,)),
             S((T,)), S((T,)), S((T,)), S((T,)),
-            S((R,)), S((R,)),
         ],
         compiler_params=pltpu.CompilerParams(
             collective_id=0, has_side_effects=True, vmem_limit_bytes=62 * 1024 * 1024
@@ -453,6 +418,7 @@
         and hidden.shape[1] == 4
         and matrix.shape[1] == QUERY_HEADS // KVH * HEAD_WIDTH
         and (down.shape[0] * down.shape[1]) % 128 == 0
+        and down.shape[0] * 2 * KVH <= 256
         and hidden.shape[2] % (CHUNKS * 4 * 128) == 0
         and cache.shape[2] % 128 == 0
     )

time: 30.5 us -> 29.8 us (0.977)
  Pallas kernels: 27.6 us -> 27 us
    pallas_call x1, Pallas kernels: 27.6 us -> 27 us  [fused_call(): pl.pallas_call(functools.partial(fused, Dims(T, NC)), out_shape=jax.Shape...]
where the time goes in v2:
time: 29.8 us; the launch traced here: 29.7 us
  Pallas kernels  27 us (91%)
  local copies, waits for them, and re-layouts  1.39 us (5%)
  between operations  1.3 us (4%)
    pallas_call x1, Pallas kernels, fused_call(): pl.pallas_call(functools.partial(fused, Dims(T, NC)), out_shape=jax.Shape...  27 us
    unnamed x1, local copies, waits for them, and re-layouts  1.39 us

profile of v2, /device:TPU:0, one launch (start us, length us, event | category | flops | bytes accessed | tf_op | source)
XLA Modules:
  0.0 29.7 jit_solution(17387546296684423556)
XLA Ops:
  1.3 27.0 %shard_map.91 = bf16[1,4,4096]{2,1,0:T(4,128)(2,1)} custom-call(bf16[1,4,8192]{2,1,0:T(4,128)(2,1)} %hidden_ref.1, bf16[8192,1024]{1,0:T(8,128)(2,1)} %matrix_ref.1, bf16[4,64,8192]{2,1,0:T(8,128)(2,1)} %down_ref.1, bf16[4,64,4096]{2,1,0:T(8,128)(2,1)} %up_ref.1, s32[1]{0:T(128)S(6)} %copy.11.adapter_ref, s32[32]{0:T(128)} %table_ref.1, ...), custom_call_target="tpu_custom_call" | custom-call | flops 1000000000 | bytes 16000000 | tf_op jit(solution)/shard_map/pallas_call | solution.py:378
  28.3 1.4 %copy.13 = bf16[1,4,4096]{2,1,0:T(4,128)(2,1)} copy(bf16[1,4,4096]{2,1,0:T(4,128)(2,1)} %shard_map.91) | data formatting | bytes 65536

commit v3 on v2

--- a/solution.py
+++ b/solution.py
@@ -331,25 +331,32 @@
     step_of = lax.rem(lax.broadcasted_iota(jnp.int32, (heads, 128), 0), steps)
     new_ok = lax.broadcasted_iota(jnp.int32, (heads, 128), 1) <= step_of
     nt = (((1,), (1,)), ((), ()))
+    lanes_of = [slice(k * HEAD_WIDTH, (k + 1) * HEAD_WIDTH) for k in range(T)]
+    olds, news = [], []
     for k in range(T):
         rows_k = queries[k * steps : (k + 1) * steps]
         qk = jnp.concatenate(
             [rows_k[:, g * HEAD_WIDTH : (g + 1) * HEAD_WIDTH] for g in range(groups)], axis=0
         ).astype(jnp.bfloat16)
-        cols = slice(k * HEAD_WIDTH, (k + 1) * HEAD_WIDTH)
-        old = lax.dot_general(qk, cache_v[0, :, cols], nt, preferred_element_type=jnp.float32) * scale
-        new = lax.dot_general(qk, fresh_keys[:, cols], nt, preferred_element_type=jnp.float32) * scale
-        old = jnp.where(old_ok, old, -1e30)
-        new = jnp.where(new_ok, new, -1e30)
-        top = jnp.maximum(jnp.max(old, axis=1, keepdims=True), jnp.max(new, axis=1, keepdims=True))
-        old = jnp.exp(old - top)
-        new = jnp.exp(new - top)
-        den = jnp.sum(old, axis=1, keepdims=True) + jnp.sum(new, axis=1, keepdims=True)
-        inv = 1.0 / den
-        res = jnp.dot((old * inv).astype(jnp.bfloat16), cache_v[1, :, cols], preferred_element_type=jnp.float32)
-        res += jnp.dot((new * inv).astype(jnp.bfloat16), fresh_vals[:, cols], preferred_element_type=jnp.float32)
-        flat = jnp.concatenate([res[g * steps : (g + 1) * steps] for g in range(groups)], axis=1)
-        out_ref[0, :, k * span : (k + 1) * span] = flat.astype(jnp.bfloat16)
+        old = lax.dot_general(qk, cache_v[0, :, lanes_of[k]], nt, preferred_element_type=jnp.float32) * scale
+        new = lax.dot_general(qk, fresh_keys[:, lanes_of[k]], nt, preferred_element_type=jnp.float32) * scale
+        olds.append(jnp.where(old_ok, old, -1e30))
+        news.append(jnp.where(new_ok, new, -1e30))
+    old = jnp.concatenate(olds, axis=0)
+    new = jnp.concatenate(news, axis=0)
+    top = jnp.maximum(jnp.max(old, axis=1, keepdims=True), jnp.max(new, axis=1, keepdims=True))
+    old = jnp.exp(old - top)
+    new = jnp.exp(new - top)
+    inv = 1.0 / (jnp.sum(old, axis=1, keepdims=True) + jnp.sum(new, axis=1, keepdims=True))
+    old = (old * inv).astype(jnp.bfloat16)
+    new = (new * inv).astype(jnp.bfloat16)
+    sums = []
+    for k in range(T):
+        here = slice(k * heads, (k + 1) * heads)
+        res = jnp.dot(old[here], cache_v[1, :, lanes_of[k]], preferred_element_type=jnp.float32)
+        res += jnp.dot(new[here], fresh_vals[:, lanes_of[k]], preferred_element_type=jnp.float32)
+        sums += [res[g * steps : (g + 1) * steps] for g in range(groups)]
+    out_ref[0] = jnp.concatenate(sums, axis=1).astype(jnp.bfloat16)
 
     for x in pending:
         x.wait_send()

time: 29.8 us -> 28.9 us (0.970)
  Pallas kernels: 27 us -> 26 us
    pallas_call x1, Pallas kernels: 27 us -> 26 us  [fused_call(): pl.pallas_call(functools.partial(fused, Dims(T, NC)), out_shape=jax.Shape...]
where the time goes in v3:
time: 28.9 us; the launch traced here: 28.7 us
  Pallas kernels  26 us (90%)
  local copies, waits for them, and re-layouts  1.39 us (5%)
  between operations  1.3 us (4%)
    pallas_call x1, Pallas kernels, fused_call(): pl.pallas_call(functools.partial(fused, Dims(T, NC)), out_shape=jax.Shape...  26 us
    unnamed x1, local copies, waits for them, and re-layouts  1.39 us

profile of v3, /device:TPU:0, one launch (start us, length us, event | category | flops | bytes accessed | tf_op | source)
XLA Modules:
  0.0 28.7 jit_solution(1784367931877588299)
XLA Ops:
  1.3 26.0 %shard_map.91 = bf16[1,4,4096]{2,1,0:T(4,128)(2,1)} custom-call(bf16[1,4,8192]{2,1,0:T(4,128)(2,1)} %hidden_ref.1, bf16[8192,1024]{1,0:T(8,128)(2,1)} %matrix_ref.1, bf16[4,64,8192]{2,1,0:T(8,128)(2,1)} %down_ref.1, bf16[4,64,4096]{2,1,0:T(8,128)(2,1)} %up_ref.1, s32[1]{0:T(128)S(6)} %copy.11.adapter_ref, s32[32]{0:T(128)} %table_ref.1, ...), custom_call_target="tpu_custom_call" | custom-call | flops 1000000000 | bytes 16000000 | tf_op jit(solution)/shard_map/pallas_call | solution.py:385
  27.3 1.4 %copy.13 = bf16[1,4,4096]{2,1,0:T(4,128)(2,1)} copy(bf16[1,4,4096]{2,1,0:T(4,128)(2,1)} %shard_map.91) | data formatting | bytes 65536

commit v4 on v3

--- a/solution.py
+++ b/solution.py
@@ -298,7 +298,7 @@
     def block_of(r):
         return jnp.concatenate([d[r * steps : (r + 1) * steps] for d in deltas], axis=0)
 
-    order_j = list(range(1, T)) + [0]
+    order_j = sorted(range(1, T), key=lambda j: abs(2 * j - T)) + [0]
     xc, dc = {}, {}
     for j in order_j:
         exch_out[j] = (block_of(2 * j + 1)).astype(LINK)

time: 28.9 us -> 28.9 us (level)
  no operation moved by 1% of the time
where the time goes in v4:
time: 28.9 us; the launch traced here: 28.7 us
  Pallas kernels  26 us (90%)
  local copies, waits for them, and re-layouts  1.39 us (5%)
  between operations  1.3 us (4%)
    pallas_call x1, Pallas kernels, fused_call(): pl.pallas_call(functools.partial(fused, Dims(T, NC)), out_shape=jax.Shape...  26 us
    unnamed x1, local copies, waits for them, and re-layouts  1.39 us

profile of v4, /device:TPU:0, one launch (start us, length us, event | category | flops | bytes accessed | tf_op | source)
XLA Modules:
  0.0 28.7 jit_solution(18007491432505904222)
XLA Ops:
  1.3 26.0 %shard_map.91 = bf16[1,4,4096]{2,1,0:T(4,128)(2,1)} custom-call(bf16[1,4,8192]{2,1,0:T(4,128)(2,1)} %hidden_ref.1, bf16[8192,1024]{1,0:T(8,128)(2,1)} %matrix_ref.1, bf16[4,64,8192]{2,1,0:T(8,128)(2,1)} %down_ref.1, bf16[4,64,4096]{2,1,0:T(8,128)(2,1)} %up_ref.1, s32[1]{0:T(128)S(6)} %copy.11.adapter_ref, s32[32]{0:T(128)} %table_ref.1, ...), custom_call_target="tpu_custom_call" | custom-call | flops 1000000000 | bytes 16000000 | tf_op jit(solution)/shard_map/pallas_call | solution.py:385
  27.3 1.4 %copy.13 = bf16[1,4,4096]{2,1,0:T(4,128)(2,1)} copy(bf16[1,4,4096]{2,1,0:T(4,128)(2,1)} %shard_map.91) | data formatting | bytes 65536
